TPU v7x, 256 devices: a whole 4x4x8 slice. The times are simulated.
256 devices in a mesh: ctx: 32 (over x, z_hi, y), exp: 8 (over z_lo, core).
Axes of the slice: x: 4, y: 4, z: 8 (z_hi: 2, z_lo: 4; z = z_hi * 4 + z_lo), core: 2. Of those that a mesh axis runs over, the one named last changes fastest.
Arguments:
- queries: bfloat16 [4096, 6144], P('ctx', 'exp'), may hold values from -8 to 8
- keys: bfloat16 [4096, 1024], P('ctx', 'exp'), may hold values from -8 to 8
- values: bfloat16 [4096, 1024], P('ctx', 'exp'), may hold values from -6 to 6
- span_order: int32 [64], replicated, may hold values from 0 to 63, each once
- norm_gain: bfloat16 [6144], replicated, may hold values from 0.099609375 to 1.8984375
- router_weight: bfloat16 [6144, 8], replicated, may hold values from -0.078125 to 0.078125
- routes: int32 [4096, 2], P(('ctx', 'exp')), may hold values from 0 to 7, all different within a row
- priority: int32 [256, 32], P(('ctx', 'exp')), may hold values from 0 to 31, each once within a row
- w_gate: bfloat16 [8, 6144, 8192], P('exp', None, 'ctx'), may hold values from -0.078125 to 0.078125
- w_up: bfloat16 [8, 6144, 8192], P('exp', None, 'ctx'), may hold values from -0.078125 to 0.078125
- w_down: bfloat16 [8, 8192, 6144], P('exp', 'ctx'), may hold values from -0.0625 to 0.0625
Outputs:
- layer_out: bfloat16 [4096, 6144], P(('ctx', 'exp'))
Inputs may be any that keep to these rules, and one draw needn't show every extreme that they name: `routes`: each token names two different experts. `priority`: each row is a permutation of 0 to 31. `span_order`: A permutation of 0 to 63.
All inputs are finite; a program needn't handle non-finite values.
Results may differ from a plain program's by a relative error of at most 0.02.
Values may be sent and summed in bfloat16 or wider, within the bound.
A program may use at most 128 MiB of HBM per device.

v0:
```python
import jax
import jax.numpy as jnp
from jax import lax
from jax.sharding import PartitionSpec as P

HD = 128


eps_norm = 1e-05
masked_score = -1e30


def passed_along(value, axis, steps):
    count = lax.axis_size(axis)
    pairs = [(source, (source + steps) % count) for source in range(count)]
    return lax.ppermute(value, axis, pairs)


def row_positions(span_order, offset, row_count, span_size):
    row_index = offset + jnp.arange(row_count, dtype=jnp.int32)
    span_ids = jnp.arange(span_order.shape[0], dtype=jnp.int32)
    matches = (row_index // span_size)[:, None] == span_ids[None, :]
    leading = jnp.sum(jnp.where(matches, span_order[None, :], 0), axis=1)
    return leading * span_size + row_index % span_size


def attend_local(query_rows, key_rows, value_rows, query_pos, key_pos, kv_local, group_size):
    row_count = query_rows.shape[0]
    key_count = key_rows.shape[0]
    query_heads = query_rows.reshape(row_count, kv_local, group_size, HD)
    key_heads = key_rows.reshape(key_count, kv_local, HD)
    value_heads = value_rows.reshape(key_count, kv_local, HD)
    scores = jnp.einsum(
        "tjgd,kjd->jgtk", query_heads, key_heads, preferred_element_type=jnp.float32
    ) * HD ** (-0.5)
    visible = (key_pos[None, :] <= query_pos[:, None])[None, None]
    scores = jnp.where(visible, scores, masked_score)
    highest = jnp.max(scores, axis=3, keepdims=True)
    weights = jnp.where(visible, jnp.exp(scores - highest), 0.0)
    denominator = jnp.sum(weights, axis=3)
    weighted = jnp.einsum(
        "jgtk,kjd->jgtd",
        weights.astype(jnp.bfloat16),
        value_heads,
        preferred_element_type=jnp.float32,
    )
    heads_out = weighted / denominator[..., None]
    return (
        heads_out.transpose(2, 0, 1, 3)
        .reshape(row_count, kv_local * group_size * HD)
        .astype(jnp.bfloat16)
    )


def pair_slots(route_rows, order_row, capacity):
    pair_expert = route_rows.reshape(-1)
    same_expert = pair_expert[:, None] == pair_expert[None, :]
    earlier = order_row[None, :] < order_row[:, None]
    pair_rank = jnp.sum((same_expert & earlier).astype(jnp.int32), axis=1)
    return (pair_expert * capacity + pair_rank, pair_rank < capacity)


def route_tables(route_rows, order_row, logit_rows, capacity, expert_layers):
    row_count = route_rows.shape[0]
    slot_index, kept_pairs = pair_slots(route_rows, order_row, capacity)
    columns = jnp.arange(expert_layers * capacity, dtype=jnp.int32)
    onehot = ((slot_index[:, None] == columns[None, :]) & kept_pairs[:, None]).astype(jnp.float32)
    onehot = onehot.reshape(row_count, 2, expert_layers * capacity)
    expert_ids = jnp.arange(expert_layers, dtype=jnp.int32)
    picked = jnp.sum(
        jnp.where(route_rows[:, :, None] == expert_ids[None, None, :], logit_rows[:, None, :], 0.0),
        axis=2,
    )
    shares = jax.nn.sigmoid(picked - picked[:, ::-1])
    return (jnp.sum(onehot, axis=1), jnp.sum(onehot * shares[:, :, None], axis=1))


def body(
    queries,
    keys,
    values,
    span_order,
    norm_gain,
    router_weight,
    routes,
    priority,
    w_gate,
    w_up,
    w_down,
):
    tokens = queries.shape[0]
    local_width = queries.shape[1]
    kv_local = keys.shape[1] // HD
    group_size = local_width // HD // kv_local
    span_size = tokens // 2
    cycle_size = lax.axis_size("ctx")
    exp_size = lax.axis_size("exp")
    block_here = lax.axis_index("ctx")
    paired = jnp.stack((keys, values))
    received = []
    current = paired
    for step in range(2):
        current = passed_along(current, "ctx", 1)
        received.append(current)
    near_pair = received[0]
    far_pair = received[1]
    window = jnp.concatenate((far_pair, near_pair, paired), axis=1)
    far_offset = (block_here - 2) % cycle_size * tokens
    neighbor_shift = (block_here - 1) % cycle_size * tokens
    query_pos = row_positions(span_order, block_here * tokens, tokens, span_size)
    key_pos = jnp.concatenate(
        (
            row_positions(span_order, far_offset, tokens, span_size),
            row_positions(span_order, neighbor_shift, tokens, span_size),
            query_pos,
        )
    )
    heads_here = attend_local(
        queries, window[0], window[1], query_pos, key_pos, kv_local, group_size
    )
    attended = lax.all_to_all(heads_here, "exp", split_axis=0, concat_axis=1, tiled=True)
    model_width = attended.shape[1]
    activations = attended.astype(jnp.float32)
    inverse_rms = lax.rsqrt(jnp.mean(activations * activations, axis=1, keepdims=True) + eps_norm)
    normed = (activations * inverse_rms * norm_gain.astype(jnp.float32)).astype(jnp.bfloat16)
    logits = jnp.dot(normed, router_weight, preferred_element_type=jnp.float32)
    expert_layers = router_weight.shape[1]
    row_count = routes.shape[0]
    capacity = max(2, 2 * row_count // expert_layers)
    slot_total = expert_layers * capacity
    dispatch_mask, combine_weights = route_tables(
        routes, priority[0], logits, capacity, expert_layers
    )
    buffer = jnp.dot(
        dispatch_mask.T.astype(jnp.bfloat16), normed, preferred_element_type=jnp.float32
    ).astype(jnp.bfloat16)
    gate_weight = w_gate[0]
    up_weight = w_up[0]
    down_weight = w_down[0]
    arrived = lax.all_to_all(
        buffer.reshape(expert_layers, capacity, model_width),
        "exp",
        split_axis=0,
        concat_axis=0,
        tiled=True,
    )
    portion = lax.all_gather(
        arrived.reshape(exp_size * capacity, model_width), "ctx", axis=0, tiled=True
    )
    gate_part = jnp.dot(portion, gate_weight, preferred_element_type=jnp.float32)
    up_part = jnp.dot(portion, up_weight, preferred_element_type=jnp.float32)
    hidden = (jax.nn.silu(gate_part) * up_part).astype(jnp.bfloat16)
    summed = lax.psum_scatter(
        jnp.dot(hidden, down_weight, preferred_element_type=jnp.float32).astype(jnp.bfloat16),
        "ctx",
        scatter_dimension=0,
        tiled=True,
    )
    returned_output = lax.all_to_all(
        summed.reshape(exp_size, capacity, model_width),
        "exp",
        split_axis=0,
        concat_axis=0,
        tiled=True,
    )
    returned_output = returned_output.reshape(slot_total, model_width)
    expert_blend = jnp.dot(
        combine_weights, returned_output.astype(jnp.float32), precision=lax.Precision.HIGHEST
    )
    return (activations + expert_blend).astype(jnp.bfloat16)


def solution(mesh):
    placed = (
        P("ctx", "exp"),
        P("ctx", "exp"),
        P("ctx", "exp"),
        P(),
        P(),
        P(),
        P(("ctx", "exp"), None),
        P(("ctx", "exp"), None),
        P("exp", None, "ctx"),
        P("exp", None, "ctx"),
        P("exp", "ctx", None),
    )
    return jax.shard_map(
        body, mesh=mesh, in_specs=placed, out_specs=P(("ctx", "exp"), None), check_vma=False
    )
```

profile of v0, /device:TPU:1, one launch (start us, length us, event | category | flops | bytes accessed | tf_op | source)
XLA Modules:
  0.0 633.9 jit_solution(5537846298712822172)
XLA Ops:
  6.5 0.9 pad_maximum_fusion
  7.5 2.2 collective-permute-start
  9.7 0.8 select_reduce_fusion.2
  10.6 0.8 copy.44
  11.5 10.2 %collective-permute-done = bf16[2,128,128]{2,1,0:T(8,128)(2,1)S(1)} collective-permute-done((bf16[2,128,128]{2,1,0:T(8,128)(2,1)S(1)}, bf16[2,128,128]{2,1,0:T(8,128)(2,1)S(1)}, u32[]{:S(2)}, u32[]{:S(2)}) %collective-permute-start) | collective-permute-done | bytes 65568 | tf_op jit(solution)/shard_map/ppermute | solution.py:16
  21.6 0.9 convert_reduce_fusion.1
  22.7 1.3 convert_element_type.69
  24.0 1.1 copy.39
  25.1 7.7 %collective-permute-done.1 = bf16[2,128,128]{2,1,0:T(8,128)(2,1)S(1)} collective-permute-done((bf16[2,128,128]{2,1,0:T(8,128)(2,1)S(1)}, bf16[2,128,128]{2,1,0:T(8,128)(2,1)S(1)}, u32[]{:S(2)}, u32[]{:S(2)}) %collective-permute-start.1) | collective-permute-done | bytes 65568 | tf_op jit(solution)/shard_map/ppermute | solution.py:16
  32.9 0.8 maximum_maximum_fusion
  33.7 0.3 fusion.40
  34.0 0.2 fusion.23
  34.2 0.4 fusion.17
  34.8 0.9 convert_element_type.63
  35.7 7.4 %all-to-all-start = ((bf16[8,16,768]{2,1,0:T(8,128)(2,1)}), bf16[8,16,768]{2,1,0:T(8,128)(2,1)S(1)}, u32[]{:S(2)}, u32[]{:S(2)}) async-start(bf16[8,16,768]{2,1,0:T(8,128)(2,1)} %convert_element_type.63), calls=%async_computation | async-start | bytes 393216 | tf_op jit(solution)/shard_map/all_to_all | solution.py:121
  43.2 0.6 broadcast_compare_fusion.1
  43.8 5.9 all-to-all-done
  49.9 1.1 fusion.39
  51.1 0.8 convert_reduce_fusion
  51.9 1.8 convolution_convert_fusion.1
  53.6 1.9 reshape.203
  55.5 17.7 %all_to_all.20 = bf16[8,4,6144]{2,1,0:T(4,128)(2,1)} all-to-all(bf16[8,4,6144]{2,1,0:T(4,128)(2,1)} %reshape.203), channel_id=1, replica_groups=mesh['ctx'=32,'exp'=8] {'exp'}, dimensions={0} | all-to-all | bytes 786432 | tf_op jit(solution)/shard_map/all_to_all | solution.py:140
  73.2 1.9 reshape.204
  75.1 0.2 reduce-scatter.2.cloned.1.call-start
  75.3 193.8 %all-gather.2.cloned.1.call-done = bf16[1024,6144]{1,0:T(8,128)(2,1)} async-done(((bf16[32,6144]{1,0:T(8,128)(2,1)}), bf16[1024,6144]{1,0:T(8,128)(2,1)}) %all-gather.2.cloned.1.call-update) | async-done | bytes 12582928 | tf_op jit(solution)/shard_map/all_gather | solution.py:147
  269.1 9.9 %fusion.4 = f32[1024,256]{1,0:T(8,128)} fusion(bf16[1024,6144]{1,0:T(8,128)(2,1)} %all-gather.2.cloned.1.call-done, bf16[1,6144,256]{2,1,0:T(8,128)(2,1)} %param.19), kind=kOutput, calls=%fused_computation.7 | convolution fusion | flops 3221225472 | bytes 16777216 | tf_op jit(solution)/shard_map/dot_general | solution.py:150
  279.0 19.8 %convolution_convert_fusion = bf16[1024,6144]{1,0:T(8,128)(2,1)} fusion(bf16[1,256,6144]{2,1,0:T(8,128)(2,1)S(1)} %copy-done, bf16[1024,6144]{1,0:T(8,128)(2,1)} %all-gather.2.cloned.1.call-done, bf16[1,6144,256]{2,1,0:T(8,128)(2,1)} %param.20, f32[1024,256]{1,0:T(8,128)} %fusion.4), kind=kOutput, calls=%fused_computation | convolution fusion | flops 6450315264 | bytes 32505856 | tf_op jit(solution)/shard_map/dot_general | solution.py:154
  298.8 304.5 %reduce-scatter.2.cloned.1.call-done = bf16[32,6144]{1,0:T(8,128)(2,1)} async-done(((bf16[1024,6144]{1,0:T(8,128)(2,1)}), bf16[32,6144]{1,0:T(8,128)(2,1)}) %reduce-scatter.2.cloned.1.call-update) | async-done | bytes 393232 | tf_op jit(solution)/shard_map/reduce_scatter | solution.py:153
  603.4 1.9 reshape.205
  605.2 18.0 %all_to_all.21 = bf16[8,4,6144]{2,1,0:T(4,128)(2,1)} all-to-all(bf16[8,4,6144]{2,1,0:T(4,128)(2,1)} %reshape.205), channel_id=1, replica_groups=mesh['ctx'=32,'exp'=8] {'exp'}, dimensions={0} | all-to-all | bytes 786432 | tf_op jit(solution)/shard_map/all_to_all | solution.py:159
  623.2 1.8 reshape.206
  625.1 2.0 fusion
  (27 shorter events, 0.9 us)
Async XLA Ops:
  6.5 272.5 %copy-start = (bf16[1,256,6144]{2,1,0:T(8,128)(2,1)S(1)}, bf16[1,256,6144]{2,1,0:T(8,128)(2,1)}, u32[]{:S(2)}) copy-start(bf16[1,256,6144]{2,1,0:T(8,128)(2,1)} %param.21) | copy-start | bytes 9437188
  7.5 14.2 %collective-permute-start = (bf16[2,128,128]{2,1,0:T(8,128)(2,1)S(1)}, bf16[2,128,128]{2,1,0:T(8,128)(2,1)S(1)}, u32[]{:S(2)}, u32[]{:S(2)}) collective-permute-start(bf16[2,128,128]{2,1,0:T(8,128)(2,1)S(1)} %pad_maximum_fusion), channel_id=1, source_target_pairs={{0,8},{8,16},{16,24},{24,32},{32,40},{40,48},{48,56},{56,64},{64,7... | collective-permute-start | bytes 196616 | tf_op jit(solution)/shard_map/ppermute | solution.py:16
  21.6 11.2 %collective-permute-start.1 = (bf16[2,128,128]{2,1,0:T(8,128)(2,1)S(1)}, bf16[2,128,128]{2,1,0:T(8,128)(2,1)S(1)}, u32[]{:S(2)}, u32[]{:S(2)}) collective-permute-start(bf16[2,128,128]{2,1,0:T(8,128)(2,1)S(1)} %collective-permute-done), channel_id=1, source_target_pairs={{0,8},{8,16},{16,24},{24,32},{32,40},{40,48},{48,56},{56,64},{64,7... | collective-permute-start | bytes 196616 | tf_op jit(solution)/shard_map/ppermute | solution.py:16
  33.7 10.1 %copy-start.1 = (s32[16,2]{0,1:T(2,128)S(1)}, s32[16,2]{0,1:T(2,128)}, u32[]{:S(2)}) copy-start(s32[16,2]{0,1:T(2,128)} %param.17) | copy-start | bytes 388
  35.7 13.9 %all-to-all-start = ((bf16[8,16,768]{2,1,0:T(8,128)(2,1)}), bf16[8,16,768]{2,1,0:T(8,128)(2,1)S(1)}, u32[]{:S(2)}, u32[]{:S(2)}) async-start(bf16[8,16,768]{2,1,0:T(8,128)(2,1)} %convert_element_type.63), calls=%async_computation | async-start | bytes 393216 | tf_op jit(solution)/shard_map/all_to_all | solution.py:121
  43.1 225.9 %all-gather.2.cloned.1.call-start = ((), (), s32[]{:S(2)}) async-start(), calls=%async_computation.4 | async-start | bytes 12976128 | tf_op jit(solution)/shard_map/all_gather | solution.py:147
  75.1 528.3 %reduce-scatter.2.cloned.1.call-start = ((), (), s32[]{:S(2)}) async-start(), calls=%async_computation.5 | async-start | bytes 12976128 | tf_op jit(solution)/shard_map/reduce_scatter | solution.py:153
Sparse Core Ops, SparseCore 0:
  75.2 193.8 all-gather.1
  298.9 304.3 reduce-scatter.1
where the time goes:
time: 635 us; the launch traced here: 634 us
  waiting for transfers between devices  522 us (82%)
  blocking collectives  35.6 us (6%)
  matrix products  35.4 us (6%)
  between operations  13.5 us (2%)
  local copies, waits for them, and re-layouts  10.7 us (2%)
  starting transfers between devices  9.83 us (2%)
  other arithmetic  6.74 us (1%)
    reduce_scatter x1, waiting for transfers between devices, body(): lax.psum_scatter(jnp.dot(hidden, down_weight, preferred_element_type=jnp....  305 us
    all_gather x1, waiting for transfers between devices, body(): lax.all_gather(arrived.reshape(exp_size * capacity, model_width), 'ctx',...  194 us
    dot_general x1, matrix products, body(): jnp.dot(hidden, down_weight, preferred_element_type=jnp.float32)  19.8 us
    all_to_all x1, blocking collectives, body(): lax.all_to_all(summed.reshape(exp_size, capacity, model_width), 'exp', sp...  18 us
    ppermute x2, waiting for transfers between devices, passed_along(): return lax.ppermute(value, axis, pairs)  17.9 us
    all_to_all x1, blocking collectives, body(): lax.all_to_all(buffer.reshape(expert_layers, capacity, model_width), 'exp...  17.7 us
  transfers between devices with their start and end apart: 5, of which 5 were waited for; matrix products, arithmetic and copies ran while one was open for 1% of the time, Pallas kernels for 0%

commit v1 on v0

v1 whole, which is shorter than its diff:
```python
import jax
import jax.numpy as jnp
from jax import lax
from jax.experimental import pallas as pl
from jax.experimental.pallas import tpu as pltpu
from jax.sharding import PartitionSpec as P

MESH = pl.DeviceIdType.MESH
BF = jnp.bfloat16
F32 = jnp.float32

HD = 128
HEADS_HERE = 6
TOK = 128
ROWS = 16
SPAN = 64
D = 6144
COLS = 768
EXP = 8
CTX = 32
CAP = 4
PARTS = 4
WIDE = D // PARTS
HID = 256
EPS = 1e-05
MASKED = -1e30


def dot(a, b):
    return jnp.dot(a, b, preferred_element_type=F32)


def kernel(
    q_ref, k_ref, v_ref, span_ref, gain_ref, router_hbm, routes_ref, prio_ref,
    gate_hbm, up_hbm, down_hbm,
    out_ref,
    kv, heads, held, router, normed, sends, arrived, tokens, gate_w, up_w, down_w,
    gate_acc, up_acc, parts, landed, back, returned, logits_ref,
    kv_s, kv_r, hd_s, hd_r, ds_s, ds_r, ag_s, ag_r, rs_s, rs_r, rt_s, rt_r, w_sem,
):
    ctx = lax.axis_index("ctx")
    me = lax.axis_index("exp")
    y = lax.rem(ctx, 4)
    zh = lax.rem(lax.div(ctx, 4), 2)
    x = lax.div(ctx, 8)

    def ctx_at(xx, zz, yy):
        return (xx * 2 + zz) * 4 + yy

    def near(axis, sign):
        step = 1 if sign > 0 else 3
        if axis == "x":
            return (ctx_at(lax.rem(x + step, 4), zh, y), me)
        return (ctx_at(x, zh, lax.rem(y + step, 4)), me)

    other_ctx = ctx_at(x, 1 - zh, y)

    def ring(far, d):
        return (other_ctx if far else ctx, lax.rem(me + d, EXP))

    def after(steps):
        return (lax.rem(ctx + steps + CTX, CTX), me)

    def remote(src, dst, s, r, device):
        return pltpu.make_async_remote_copy(
            src_ref=src, dst_ref=dst, send_sem=s, recv_sem=r,
            device_id=device, device_id_type=MESH,
        )

    weight_copies = [
        pltpu.make_async_copy(router_hbm, router, w_sem.at[0]),
        pltpu.make_async_copy(gate_hbm.at[0], gate_w, w_sem.at[1]),
        pltpu.make_async_copy(up_hbm.at[0], up_w, w_sem.at[2]),
        pltpu.make_async_copy(down_hbm.at[0], down_w, w_sem.at[3]),
    ]

    barrier = pltpu.get_barrier_semaphore()
    greeted = [after(-1), after(-2)]
    greeted += [near(axis, sign) for axis in "xy" for sign in (1, -1)]
    greeted += [ring(far, d) for far in (0, 1) for d in range(EXP) if far or d]
    for device in greeted:
        pl.semaphore_signal(barrier, inc=1, device_id=device, device_id_type=MESH)
    pl.semaphore_wait(barrier, len(greeted))

    kv_copies = []
    for back_steps in (1, 2):
        for which, ref in enumerate((k_ref, v_ref)):
            slot = (back_steps - 1) * 2 + which
            copy = remote(ref, kv.at[slot], kv_s.at[slot], kv_r.at[slot], after(back_steps))
            copy.start()
            kv_copies.append(copy)
    for copy in weight_copies:
        copy.start()

    def span_base(block, half):
        return span_ref[block * 2 + half] * SPAN

    blocks = [lax.rem(ctx + CTX - 2, CTX), lax.rem(ctx + CTX - 1, CTX), ctx]
    lane = lax.broadcasted_iota(jnp.int32, (TOK, 3 * TOK), 1)
    sub = lax.broadcasted_iota(jnp.int32, (TOK, 3 * TOK), 0)
    key_pos = lax.rem(lane, SPAN)
    lane_span = lax.div(lane, SPAN)
    for n in range(6):
        key_pos = key_pos + jnp.where(lane_span == n, span_base(blocks[n // 2], n % 2), 0)
    query_pos = lax.rem(sub, SPAN) + jnp.where(
        sub < SPAN, span_base(ctx, 0), span_base(ctx, 1)
    )
    visible = key_pos <= query_pos

    lane_t = lax.rem(lax.broadcasted_iota(jnp.int32, (ROWS, 64), 1), ROWS)
    pick = lax.broadcasted_iota(jnp.int32, (ROWS, 64), 0) == lane_t
    first = lax.broadcasted_iota(jnp.int32, (ROWS, 64), 1) < ROWS
    lane_32 = lax.broadcasted_iota(jnp.int32, (ROWS, 32), 1)
    sub_32 = lax.broadcasted_iota(jnp.int32, (ROWS, 32), 0)
    routes = routes_ref[...].astype(F32)
    prio = prio_ref[...].astype(F32)
    e_col = [routes[:, k : k + 1] for k in range(2)]
    p_col = [
        jnp.sum(jnp.where(lane_32 == 2 * sub_32 + k, prio, 0.0), axis=1, keepdims=True)
        for k in range(2)
    ]
    e_row = [jnp.sum(jnp.where(pick, e, 0.0), axis=0, keepdims=True) for e in e_col]
    p_row = [jnp.sum(jnp.where(pick, p, 0.0), axis=0, keepdims=True) for p in p_col]
    slot_row, slot_col = [], []
    for k in range(2):
        rank_row = jnp.zeros((1, 64), F32)
        rank_col = jnp.zeros((ROWS, 1), F32)
        for n in range(2):
            rank_row += jnp.sum(
                jnp.where((e_col[n] == e_row[k]) & (p_col[n] < p_row[k]), 1.0, 0.0),
                axis=0, keepdims=True,
            )
            rank_col += jnp.sum(
                jnp.where((e_row[n] == e_col[k]) & (p_row[n] < p_col[k]) & first, 1.0, 0.0),
                axis=1, keepdims=True,
            )
        slot_row.append(jnp.where(rank_row < CAP, e_row[k] * CAP + rank_row, -1.0))
        slot_col.append(jnp.where(rank_col < CAP, e_col[k] * CAP + rank_col, -1.0))

    for copy in kv_copies:
        copy.wait_recv()
    key_blocks = [kv[2], kv[0], k_ref[...]]
    value_blocks = [kv[3], kv[1], v_ref[...]]
    for h in range(HEADS_HERE):
        query = q_ref[:, h * HD : (h + 1) * HD]
        scores = jnp.concatenate(
            [
                lax.dot_general(
                    query, block, (((1,), (1,)), ((), ())), preferred_element_type=F32
                )
                for block in key_blocks
            ],
            axis=1,
        ) * HD ** (-0.5)
        scores = jnp.where(visible, scores, MASKED)
        highest = jnp.max(scores, axis=1, keepdims=True)
        weights = jnp.where(visible, jnp.exp(scores - highest), 0.0)
        denominator = jnp.sum(weights, axis=1, keepdims=True)
        weights = weights.astype(BF)
        total = dot(weights[:, :TOK], value_blocks[0])
        total += dot(weights[:, TOK : 2 * TOK], value_blocks[1])
        total += dot(weights[:, 2 * TOK :], value_blocks[2])
        head = (total / denominator).astype(BF)
        heads[:, :, h * HD : (h + 1) * HD] = head.reshape(EXP, ROWS, HD)

    head_copies = []
    for d in range(1, EXP):
        peer = lax.rem(me + d, EXP)
        copy = remote(heads.at[peer], held.at[me], hd_s.at[d], hd_r.at[d], ring(0, d))
        copy.start()
        head_copies.append(copy)
    held[me] = heads[me]

    lane_64 = lax.broadcasted_iota(jnp.int32, (128, 64), 1)
    row_128 = lax.broadcasted_iota(jnp.int32, (128, 64), 0)
    row_expert = lax.rem(lax.div(row_128, 16) + me, EXP)
    row_slot = (row_expert * CAP + lax.rem(row_128, 4)).astype(F32)
    same_part = lax.rem(lax.div(row_128, 4), 4) == lax.div(lane_64, ROWS)
    dispatch = jnp.where(
        same_part & ((slot_row[0] == row_slot) | (slot_row[1] == row_slot)), 1.0, 0.0
    ).astype(BF)
    row_64 = lax.broadcasted_iota(jnp.int32, (64, 64), 0)
    col_64 = lax.broadcasted_iota(jnp.int32, (64, 64), 1)
    swapped = lax.rem(lax.div(row_64, 4), 4) * 16 + lax.div(row_64, 16) * 4 + lax.rem(row_64, 4)
    swap = jnp.where(col_64 == swapped, 1.0, 0.0).astype(BF)

    for copy in head_copies:
        copy.wait_recv()
    square = jnp.zeros((ROWS, 1), F32)
    for e in range(EXP):
        block = held[e].astype(F32)
        square += jnp.sum(block * block, axis=1, keepdims=True)
    inverse = lax.rsqrt(square * (1.0 / D) + EPS)
    for e in range(EXP):
        block = held[e].astype(F32) * inverse * gain_ref[:, e * COLS : (e + 1) * COLS]
        q0 = e // 2
        normed[q0 * ROWS : (q0 + 1) * ROWS, (e % 2) * COLS : (e % 2 + 1) * COLS] = block.astype(BF)

    sends[...] = dot(dispatch, normed[...]).astype(BF).reshape(EXP, 16, WIDE)
    slot_copies = {}
    for far in (0, 1):
        for d in range(EXP):
            if not far and not d:
                continue
            n = far * EXP + (EXP - d) % EXP
            copy = remote(sends.at[d], arrived.at[n], ds_s.at[n], ds_r.at[n], ring(far, d))
            copy.start()
            slot_copies[n] = copy
    arrived[0] = sends[0]

    weight_copies[0].wait()
    logits = jnp.zeros((ROWS, EXP), F32)
    for e in range(EXP):
        q0 = e // 2
        block = normed[q0 * ROWS : (q0 + 1) * ROWS, (e % 2) * COLS : (e % 2 + 1) * COLS]
        logits += dot(block, router[e * COLS : (e + 1) * COLS, :])
    lane_8 = lax.broadcasted_iota(jnp.int32, (ROWS, EXP), 1).astype(F32)
    picked = [
        jnp.sum(jnp.where(lane_8 == e, logits, 0.0), axis=1, keepdims=True) for e in e_col
    ]
    shares = [
        1.0 / (1.0 + jnp.exp(picked[1] - picked[0])),
        1.0 / (1.0 + jnp.exp(picked[0] - picked[1])),
    ]
    lane_256 = lax.broadcasted_iota(jnp.int32, (64, 256), 1)
    row_b = lax.broadcasted_iota(jnp.int32, (64, 256), 0)
    lane_expert = lax.rem(me + EXP - lax.rem(lax.div(lane_256, 16), EXP), EXP)
    lane_slot = (lane_expert * CAP + lax.rem(lane_256, 4)).astype(F32)
    blend = jnp.zeros((64, 256), F32)
    for k in range(2):
        slot_tall = jnp.concatenate([slot_col[k]] * PARTS, axis=0)
        share_tall = jnp.concatenate([shares[k]] * PARTS, axis=0)
        blend += jnp.where(slot_tall == lane_slot, share_tall, 0.0)
    blend = jnp.where(lax.div(row_b, ROWS) == lax.rem(lax.div(lane_256, 4), 4), blend, 0.0)
    logits_ref[...] = blend

    axes = [("x", "y"), ("y", "x"), ("x", "y"), ("y", "x")]
    first_sign = [1, -1, -1, 1]

    def second_sign(a):
        return 1 if a < 2 else -1

    ag = [dict() for _ in range(4)]

    def at(a, b):
        return a * 4 + b

    def push(k, src, dst, axis, sign):
        copy = remote(
            tokens.at[k, src], tokens.at[k, dst], ag_s.at[k, dst], ag_r.at[k, dst],
            near(axis, sign),
        )
        copy.start()
        ag[k][dst] = copy

    def take_slots(k):
        for m in range(4):
            n = (k // 2) * EXP + (k % 2) * 4 + m
            if n:
                slot_copies[n].wait_recv()
        first_n = (k // 2) * EXP + (k % 2) * 4
        rows = arrived[first_n : first_n + 4].reshape(64, WIDE)
        moved = dot(swap, rows).astype(BF)
        for part in range(PARTS):
            tokens[k, 0, :, part * WIDE : (part + 1) * WIDE] = moved[part * 16 : (part + 1) * 16]

    def spread(k, a):
        push(k, at(a, 0), at(a, 3), axes[k][1], 1)
        push(k, at(a, 0), at(a, 1), axes[k][1], -1)

    def ag_steps(k):
        sign = first_sign[k]

        def own():
            take_slots(k)
            push(k, 0, at(3, 0), axes[k][0], 1)
            push(k, 0, at(1, 0), axes[k][0], -1)
            spread(k, 0)

        def neighbours():
            for a in (3, 1) if sign > 0 else (1, 3):
                ag[k][at(a, 0)].wait_recv()
                if a == (3 if sign > 0 else 1):
                    push(k, at(a, 0), at(2, 0), axes[k][0], sign)
                spread(k, a)

        def onward(a):
            b = 3 if second_sign(a) > 0 else 1

            def go():
                ag[k][at(a, b)].wait_recv()
                push(k, at(a, b), at(a, 2), axes[k][1], second_sign(a))

            return go

        def opposite():
            ag[k][at(2, 0)].wait_recv()
            spread(k, 2)

        def rest():
            for a in range(4):
                ag[k][at(a, 1 if second_sign(a) > 0 else 3)].wait_recv()
            for a in range(4):
                ag[k][at(a, 2)].wait_recv()

        return [own, neighbours, onward(0), opposite, onward(1), onward(3), onward(2), rest]

    def ffn_steps(k):
        def up_step(n):
            def go():
                if k == 0 and n == 0:
                    for copy in weight_copies[1:]:
                        copy.wait()
                columns = slice(n * WIDE, (n + 1) * WIDE)
                rows = tokens[k, :, :, columns].reshape(256, WIDE)
                g = dot(rows, gate_w[columns, :])
                u = dot(rows, up_w[columns, :])
                if n:
                    gate_acc[...] += g
                    up_acc[...] += u
                else:
                    gate_acc[...] = g
                    up_acc[...] = u

            return go

        def down_step(n):
            def go():
                gate = gate_acc[...]
                hidden = (gate / (1.0 + jnp.exp(-gate)) * up_acc[...]).astype(BF)
                columns = slice(n * WIDE, (n + 1) * WIDE)
                parts[k, :, :, columns] = (
                    dot(hidden, down_w[:, columns]).astype(BF).reshape(16, 16, WIDE)
                )

            return go

        return [up_step(n) for n in range(PARTS)] + [down_step(n) for n in range(PARTS)]

    rs = [dict() for _ in range(4)]

    def hand(k, src, n, axis, sign):
        copy = remote(
            parts.at[k, src], landed.at[k, n], rs_s.at[k, n], rs_r.at[k, n], near(axis, sign)
        )
        copy.start()
        rs[k][n] = copy

    def add(k, slot, *ns):
        total = parts[k, slot].astype(F32)
        for n in ns:
            total += landed[k, n].astype(F32)
        parts[k, slot] = total.astype(BF)

    rt = []

    def rs_steps(k):
        sign = first_sign[k]
        mid, opp = (1, 3) if sign > 0 else (3, 1)
        order = [2, mid, opp, 0]

        def begin():
            for a in order:
                s = second_sign(a)
                hand(k, at(a, 2), a * 3, axes[k][1], s)
                hand(k, at(a, 3 if s > 0 else 1), a * 3 + 2, axes[k][1], -s)

        def middle(a):
            def go():
                s = second_sign(a)
                m = at(a, 1 if s > 0 else 3)
                rs[k][a * 3].wait_recv()
                add(k, m, a * 3)
                hand(k, m, a * 3 + 1, axes[k][1], s)

            return go

        def close(a):
            def go():
                rs[k][a * 3 + 1].wait_recv()
                rs[k][a * 3 + 2].wait_recv()
                if a == 2:
                    add(k, at(a, 0), a * 3 + 1, a * 3 + 2)
                    hand(k, at(2, 0), 12, axes[k][0], sign)
                elif a == opp:
                    add(k, at(a, 0), a * 3 + 1, a * 3 + 2)
                    hand(k, at(opp, 0), 14, axes[k][0], -sign)
                elif a == mid:
                    rs[k][12].wait_recv()
                    add(k, at(a, 0), a * 3 + 1, a * 3 + 2, 12)
                    hand(k, at(mid, 0), 13, axes[k][0], sign)
                else:
                    rs[k][13].wait_recv()
                    rs[k][14].wait_recv()
                    add(k, at(a, 0), a * 3 + 1, a * 3 + 2, 13, 14)

            return go

        def give_back():
            rows = jnp.concatenate(
                [parts[k, 0, :, n * WIDE : (n + 1) * WIDE] for n in range(PARTS)], axis=0
            )
            back[k] = dot(swap, rows).astype(BF).reshape(4, 16, WIDE)
            for m in range(4):
                d = (k % 2) * 4 + m
                n = (k // 2) * EXP + d
                if n:
                    copy = remote(
                        back.at[k, m], returned.at[n], rt_s.at[n], rt_r.at[n], ring(k // 2, d)
                    )
                    copy.start()
                    rt.append(copy)
                else:
                    returned[0] = back[k, m]

        return (
            [begin]
            + [middle(a) for a in order]
            + [close(2), close(opp), close(mid), close(0), give_back]
        )

    def run(*lists):
        for n in range(max(len(one) for one in lists)):
            for one in lists:
                if n < len(one):
                    one[n]()

    g = [ag_steps(k) for k in range(4)]
    f = [ffn_steps(k) for k in range(4)]
    r = [rs_steps(k) for k in range(4)]
    run(g[0][:2], g[1][:2])
    run(g[2][:1], g[3][:1])
    run(g[0][2:7], g[1][2:7])
    run(g[2][1:3], g[3][1:3])
    g[0][7]()
    run(f[0], g[2][3:7], g[3][3:7])
    g[1][7]()
    run(f[1])
    run(r[0][:1], r[1][:1])
    g[2][7]()
    run(f[2], r[0][1:5])
    g[3][7]()
    run(f[3], r[1][1:5])
    run(r[2][:1], r[3][:1])
    run(r[0][5:], r[1][5:])
    run(r[2][1:], r[3][1:])

    for copy in rt:
        copy.wait_recv()
    blend = logits_ref[...]
    high = blend.astype(BF)
    low = (blend - high.astype(F32)).astype(BF)
    came = returned[...].reshape(256, WIDE)
    mixed = dot(high, came) + dot(low, came)
    for e in range(EXP):
        q0 = e // 2
        block = mixed[q0 * ROWS : (q0 + 1) * ROWS, (e % 2) * COLS : (e % 2 + 1) * COLS]
        out_ref[:, e * COLS : (e + 1) * COLS] = (held[e].astype(F32) + block).astype(BF)

    for copy in kv_copies + head_copies + list(slot_copies.values()) + rt:
        copy.wait_send()
    for k in range(4):
        for copy in list(ag[k].values()) + list(rs[k].values()):
            copy.wait_send()


def body(
    queries, keys, values, span_order, norm_gain, router_weight, routes, priority,
    w_gate, w_up, w_down,
):
    vmem = pl.BlockSpec(memory_space=pltpu.VMEM)
    smem = pl.BlockSpec(memory_space=pltpu.SMEM)
    hbm = pl.BlockSpec(memory_space=pl.ANY)
    dma = pltpu.SemaphoreType.DMA
    return pl.pallas_call(
        kernel,
        out_shape=jax.ShapeDtypeStruct((ROWS, D), BF),
        in_specs=[vmem, vmem, vmem, smem, vmem, hbm, vmem, vmem, hbm, hbm, hbm],
        out_specs=vmem,
        scratch_shapes=[
            pltpu.VMEM((4, TOK, HD), BF),
            pltpu.VMEM((EXP, ROWS, COLS), BF),
            pltpu.VMEM((EXP, ROWS, COLS), BF),
            pltpu.VMEM((D, EXP), BF),
            pltpu.VMEM((64, WIDE), BF),
            pltpu.VMEM((EXP, 16, WIDE), BF),
            pltpu.VMEM((2 * EXP, 16, WIDE), BF),
            pltpu.VMEM((4, 16, 16, D), BF),
            pltpu.VMEM((D, HID), BF),
            pltpu.VMEM((D, HID), BF),
            pltpu.VMEM((HID, D), BF),
            pltpu.VMEM((256, HID), F32),
            pltpu.VMEM((256, HID), F32),
            pltpu.VMEM((4, 16, 16, D), BF),
            pltpu.VMEM((4, 15, 16, D), BF),
            pltpu.VMEM((4, 4, 16, WIDE), BF),
            pltpu.VMEM((2 * EXP, 16, WIDE), BF),
            pltpu.VMEM((64, 256), F32),
            dma((4,)), dma((4,)),
            dma((EXP,)), dma((EXP,)),
            dma((2 * EXP,)), dma((2 * EXP,)),
            dma((4, 16)), dma((4, 16)),
            dma((4, 15)), dma((4, 15)),
            dma((2 * EXP,)), dma((2 * EXP,)),
            dma((4,)),
        ],
        compiler_params=pltpu.CompilerParams(
            collective_id=0, has_side_effects=True, vmem_limit_bytes=60 * 1024 * 1024
        ),
    )(
        queries, keys, values, span_order, norm_gain.astype(F32).reshape(1, D),
        router_weight, routes, priority, w_gate, w_up, w_down,
    )


def solution(mesh):
    placed = (
        P("ctx", "exp"),
        P("ctx", "exp"),
        P("ctx", "exp"),
        P(),
        P(),
        P(),
        P(("ctx", "exp"), None),
        P(("ctx", "exp"), None),
        P("exp", None, "ctx"),
        P("exp", None, "ctx"),
        P("exp", "ctx", None),
    )
    return jax.shard_map(
        body, mesh=mesh, in_specs=placed, out_specs=P(("ctx", "exp"), None), check_vma=False
    )
```

time: 635 us -> 211 us (0.33)
  waiting for transfers between devices: 522 us -> 0 us
  Pallas kernels: 0 us -> 204 us
  blocking collectives: 35.6 us -> 0 us
  matrix products: 35.4 us -> 0 us
  between operations: 13.5 us -> 0.01 us
  starting transfers between devices: 9.83 us -> 0 us
    reduce_scatter x1 -> x0, waiting for transfers between devices: 305 us -> none  [body(): lax.psum_scatter(jnp.dot(hidden, down_weight, preferred_element_type=jnp....]
    pallas_call x0 -> x1, Pallas kernels: none -> 204 us  [body(): pl.pallas_call(kernel, out_shape=jax.ShapeDtypeStruct((ROWS, D), BF), in_...]
    all_gather x1 -> x0, waiting for transfers between devices: 194 us -> none  [body(): lax.all_gather(arrived.reshape(exp_size * capacity, model_width), 'ctx',...]
    all_to_all x2 -> x0, blocking collectives: 35.6 us -> none  [the longest x1 18 us: body(): lax.all_to_all(summed.reshape(exp_size, capacity, model_width), 'exp', sp...]
    dot_general x7 -> x0, matrix products: 35.4 us -> none  [the longest x1 19.8 us: body(): jnp.dot(hidden, down_weight, preferred_element_type=jnp.float32)]
    ppermute x2 -> x0, waiting for transfers between devices: 17.9 us -> none  [passed_along(): return lax.ppermute(value, axis, pairs)]
    reshape x4 -> x0, local copies, waits for them, and re-layouts: 7.47 us -> none  [the longest x1 1.89 us: body(): buffer.reshape(expert_layers, capacity, model_width)]
    all_to_all x1 -> x0, starting transfers between devices: 7.41 us -> none  [body(): lax.all_to_all(heads_here, 'exp', split_axis=0, concat_axis=1, tiled=True)]
  transfers between devices with their start and end apart: 5 -> 0, of which waited for: 5 -> 0; matrix products, arithmetic and copies ran while one was open for 1% -> 0% of each run, Pallas kernels for 0% -> 0%
where the time goes in v1:
time: 211 us
  Pallas kernels  204 us (97%)
  local copies, waits for them, and re-layouts  5.23 us (2%)
    pallas_call x1, Pallas kernels, body(): pl.pallas_call(kernel, out_shape=jax.ShapeDtypeStruct((ROWS, D), BF), in_...  204 us
    unnamed x3, local copies, waits for them, and re-layouts  5.23 us

profile of v1, /device:TPU:1, one launch (start us, length us, event | category | flops | bytes accessed | tf_op | source)
XLA Modules:
  0.0 210.7 jit_solution(17127749052377226689)
XLA Ops:
  0.0 1.3 copy.13.routes_ref
  1.4 1.3 reshape.7
  2.7 2.3 %copy.12.router_hbm = bf16[6144,8]{1,0:T(8,128)(2,1)} copy(bf16[6144,8]{0,1:T(8,128)(2,1)} %param.16) | data formatting | bytes 196608 | tf_op args[5]
  4.9 204.1 %shard_map.109 = bf16[16,6144]{1,0:T(8,128)(2,1)} custom-call(bf16[128,768]{1,0:T(8,128)(2,1)} %q_ref.1, bf16[128,128]{1,0:T(8,128)(2,1)} %k_ref.1, bf16[128,128]{1,0:T(8,128)(2,1)} %v_ref.1, s32[64]{0:T(128)} %span_ref.1, f32[1,6144]{1,0:T(1,128)} %bitcast.1, bf16[6144,8]{1,0:T(8,128)(2,1)} %copy.12.router_hbm, s32[16,2]{1,0:T(8,128)} %copy.13.routes_ref, ...), custom_call_target="tpu_custom_call" | custom-call | tf_op jit(solution)/shard_map/pallas_call | solution.py:475
  209.1 1.6 copy.15

commit v2 on v1

v2 whole, which is shorter than its diff:
```python
import jax
import jax.numpy as jnp
from jax import lax
from jax.experimental import pallas as pl
from jax.experimental.pallas import tpu as pltpu
from jax.sharding import PartitionSpec as P

MESH = pl.DeviceIdType.MESH
BF = jnp.bfloat16
F32 = jnp.float32

HD = 128
HEADS_HERE = 6
TOK = 128
ROWS = 16
SPAN = 64
D = 6144
COLS = 768
EXP = 8
CTX = 32
CAP = 4
PARTS = 4
WIDE = D // PARTS
HALVES = 2
HALF = D // HALVES
NARROW = HALF // PARTS
GROUPS = 2
GROUP_HEADS = HEADS_HERE // GROUPS
GROUP_COLS = GROUP_HEADS * HD
HID = 256
CROSSING = (0, 3)
OVER = (2, 1)
ORDER = (
    (0, 0), (1, 0, 0), (2, 0), (1, 0, 3), (0, 1), (1, 1, 0), (1, 0, 1), (1, 0, 2), (3, 1, 0),
    (2, 1), (1, 1, 3), (1, 1, 1), (3, 0, 0), (0, 2), (0, 3), (1, 2, 0), (1, 3, 0), (4, 3, 0),
    (3, 1, 3), (4, 2, 0), (1, 1, 2), (3, 0, 3), (3, 0, 1), (2, 2), (1, 2, 1), (2, 3), (1, 3, 1),
    (1, 3, 3), (1, 2, 3), (4, 3, 3), (4, 2, 3), (3, 0, 2), (3, 1, 1), (3, 2, 1), (1, 2, 2),
    (3, 3, 1), (3, 1, 2), (1, 3, 2), (5, 0, 0), (5, 0, 1), (5, 0, 2), (5, 0, 3), (5, 0, 4),
    (5, 0, 5), (5, 0, 6), (5, 0, 7), (9, 0, 1, 2), (9, 0, 0, 2), (9, 0, 1, 1), (9, 0, 0, 1),
    (7, 0, 1, 3), (7, 0, 0, 3), (7, 0, 1, 0), (7, 0, 0, 0), (6, 0, 1, 2), (6, 0, 0, 2),
    (6, 0, 1, 1), (6, 0, 0, 1), (3, 2, 2), (5, 1, 0), (5, 1, 1), (5, 1, 2), (5, 1, 3), (5, 1, 4),
    (5, 1, 5), (9, 1, 0, 2), (5, 1, 6), (5, 1, 7), (9, 1, 1, 2), (9, 1, 1, 1), (9, 1, 0, 1),
    (7, 1, 1, 3), (7, 1, 0, 3), (8, 0, 1, 2), (8, 1, 1, 2), (8, 1, 0, 2), (7, 1, 1, 0),
    (7, 1, 0, 0), (8, 0, 1, 1), (6, 1, 1, 2), (6, 1, 0, 2), (6, 1, 1, 1), (6, 1, 0, 1), (3, 3, 2),
    (8, 0, 0, 2), (9, 0, 1, 3), (8, 0, 1, 3), (9, 0, 0, 3), (9, 0, 1, 0), (8, 1, 1, 1),
    (8, 1, 1, 3), (8, 0, 0, 1), (9, 1, 1, 3), (9, 0, 0, 0), (10, 1, 1, 2), (5, 2, 0), (5, 2, 1),
    (9, 1, 0, 3), (5, 2, 2), (5, 2, 3), (5, 2, 4), (5, 2, 5), (5, 2, 6), (5, 2, 7), (7, 2, 1, 2),
    (9, 1, 1, 0), (7, 2, 0, 2), (7, 2, 1, 3), (8, 1, 0, 3), (8, 0, 0, 3), (8, 1, 0, 1),
    (7, 2, 0, 3), (8, 2, 1, 2), (10, 0, 1, 2), (10, 0, 0, 2), (5, 3, 0), (5, 3, 1), (9, 1, 0, 0),
    (5, 3, 2), (5, 3, 3), (5, 3, 4), (5, 3, 5), (5, 3, 6), (5, 3, 7), (7, 2, 1, 1), (7, 3, 1, 3),
    (7, 3, 0, 3), (8, 2, 0, 2), (10, 1, 0, 2), (7, 2, 1, 0), (7, 3, 1, 0), (7, 2, 0, 0),
    (7, 3, 0, 0), (8, 1, 1, 0), (10, 0, 1, 3), (10, 1, 1, 1), (10, 1, 1, 3), (10, 0, 0, 3),
    (9, 2, 1, 2), (10, 1, 0, 1), (7, 2, 0, 1), (10, 0, 1, 1), (9, 2, 0, 2), (9, 3, 1, 3),
    (9, 2, 1, 1), (10, 0, 0, 1), (9, 2, 1, 3), (9, 3, 0, 3), (7, 3, 1, 2), (9, 2, 0, 3),
    (8, 3, 1, 2), (9, 2, 1, 0), (9, 3, 1, 0), (10, 1, 0, 3), (9, 2, 0, 0), (8, 1, 0, 0),
    (9, 3, 0, 0), (7, 3, 0, 2), (10, 1, 1, 0), (11, 1, 1), (10, 2, 1, 2), (8, 3, 0, 2),
    (8, 0, 1, 0), (8, 2, 1, 3), (10, 2, 0, 2), (8, 3, 1, 3), (8, 0, 0, 0), (9, 2, 0, 1),
    (7, 3, 1, 1), (8, 2, 1, 1), (9, 3, 1, 2), (8, 2, 0, 3), (8, 3, 0, 3), (8, 2, 0, 1),
    (8, 3, 1, 1), (10, 1, 0, 0), (11, 1, 0), (9, 3, 0, 2), (7, 3, 0, 1), (8, 2, 1, 0),
    (10, 0, 1, 0), (11, 0, 1), (8, 2, 0, 0), (10, 2, 1, 3), (10, 3, 1, 3), (10, 0, 0, 0),
    (11, 0, 0), (8, 3, 0, 1), (9, 3, 1, 1), (10, 2, 1, 1), (10, 3, 1, 2), (10, 2, 0, 3),
    (10, 3, 0, 3), (10, 2, 0, 1), (8, 3, 1, 0), (9, 3, 0, 1), (10, 3, 0, 2), (8, 3, 0, 0),
    (10, 3, 1, 1), (10, 2, 1, 0), (11, 2, 1), (10, 2, 0, 0), (11, 2, 0), (10, 3, 0, 1),
    (10, 3, 1, 0), (11, 3, 1), (10, 3, 0, 0), (11, 3, 0),
)
EPS = 1e-05
MASKED = -1e30


def dot(a, b):
    return jnp.dot(a, b, preferred_element_type=F32)


def kernel(
    q_ref, k_ref, v_ref, span_ref, gain_ref, router_ref, routes_ref, prio_ref,
    gate_hbm, up_hbm, down_hbm,
    out_ref,
    kv, own_scores, heads, held, normed, sends, arrived, tokens, gate_w, up_w, down_w,
    gate_acc, up_acc, hidden, parts, landed, crossed, back, returned, blend_ref,
    kv_s, kv_r, hd_s, hd_r, ds_s, ds_r, ag_s, ag_r, rs_s, rs_r, ov_s, ov_r, rt_s, rt_r, w_sem,
):
    ctx = lax.axis_index("ctx")
    me = lax.axis_index("exp")
    y = lax.rem(ctx, 4)
    zh = lax.rem(lax.div(ctx, 4), 2)
    x = lax.div(ctx, 8)

    def ctx_at(xx, zz, yy):
        return (xx * 2 + zz) * 4 + yy

    def near(axis, sign):
        step = 1 if sign > 0 else 3
        if axis == "x":
            return (ctx_at(lax.rem(x + step, 4), zh, y), me)
        return (ctx_at(x, zh, lax.rem(y + step, 4)), me)

    other_ctx = ctx_at(x, 1 - zh, y)

    bits = [lax.rem(me, 2), lax.rem(lax.div(me, 2), 2), lax.div(me, 4)]

    def partner(d):
        flipped = [1 - bit if d >> n & 1 else bit for n, bit in enumerate(bits)]
        return flipped[0] + 2 * flipped[1] + 4 * flipped[2]

    def ring(far, d):
        return (other_ctx if far else ctx, partner(d))

    def after(steps):
        return (lax.rem(ctx + steps + CTX, CTX), me)

    def remote(src, dst, s, r, device):
        return pltpu.make_async_remote_copy(
            src_ref=src, dst_ref=dst, send_sem=s, recv_sem=r,
            device_id=device, device_id_type=MESH,
        )

    weight_copies = [
        pltpu.make_async_copy(gate_hbm.at[0], gate_w, w_sem.at[0]),
        pltpu.make_async_copy(up_hbm.at[0], up_w, w_sem.at[1]),
        pltpu.make_async_copy(down_hbm.at[0], down_w, w_sem.at[2]),
    ]

    barrier = pltpu.get_barrier_semaphore()
    greeted = [after(-1), after(-2)]
    greeted += [ring(0, d) for d in range(1, EXP)]
    greeted += [near(axis, sign) for axis in "xy" for sign in (1, -1)]
    greeted += [ring(1, d) for d in range(EXP)]
    for device in greeted:
        pl.semaphore_signal(barrier, inc=1, device_id=device, device_id_type=MESH)

    def span_base(block, half):
        return span_ref[block * 2 + half] * SPAN

    blocks = [lax.rem(ctx + CTX - 2, CTX), lax.rem(ctx + CTX - 1, CTX), ctx]
    lane = lax.broadcasted_iota(jnp.int32, (TOK, 3 * TOK), 1)
    sub = lax.broadcasted_iota(jnp.int32, (TOK, 3 * TOK), 0)
    key_pos = lax.rem(lane, SPAN)
    lane_span = lax.div(lane, SPAN)
    for n in range(6):
        key_pos = key_pos + jnp.where(lane_span == n, span_base(blocks[n // 2], n % 2), 0)
    query_pos = lax.rem(sub, SPAN) + jnp.where(
        sub < SPAN, span_base(ctx, 0), span_base(ctx, 1)
    )
    visible = key_pos <= query_pos

    lane_t = lax.rem(lax.broadcasted_iota(jnp.int32, (ROWS, 64), 1), ROWS)
    pick = lax.broadcasted_iota(jnp.int32, (ROWS, 64), 0) == lane_t
    first = lax.broadcasted_iota(jnp.int32, (ROWS, 64), 1) < ROWS
    lane_16 = lax.broadcasted_iota(jnp.int32, (ROWS, ROWS), 1)
    sub_16 = lax.broadcasted_iota(jnp.int32, (ROWS, ROWS), 0)
    lane_32 = lax.broadcasted_iota(jnp.int32, (ROWS, 32), 1)
    sub_32 = lax.broadcasted_iota(jnp.int32, (ROWS, 32), 0)
    routes = routes_ref[...].astype(F32)
    prio = prio_ref[...].astype(F32)
    e_col = [
        jnp.sum(jnp.where(lane_16 == sub_16, routes[k : k + 1, :], 0.0), axis=1, keepdims=True)
        for k in range(2)
    ]
    p_col = [
        jnp.sum(jnp.where(lane_32 == 2 * sub_32 + k, prio, 0.0), axis=1, keepdims=True)
        for k in range(2)
    ]
    e_row = [jnp.sum(jnp.where(pick, e, 0.0), axis=0, keepdims=True) for e in e_col]
    p_row = [jnp.sum(jnp.where(pick, p, 0.0), axis=0, keepdims=True) for p in p_col]
    slot_row, slot_col = [], []
    for k in range(2):
        rank_row = jnp.zeros((1, 64), F32)
        rank_col = jnp.zeros((ROWS, 1), F32)
        for n in range(2):
            rank_row += jnp.sum(
                jnp.where((e_col[n] == e_row[k]) & (p_col[n] < p_row[k]), 1.0, 0.0),
                axis=0, keepdims=True,
            )
            rank_col += jnp.sum(
                jnp.where((e_row[n] == e_col[k]) & (p_row[n] < p_col[k]) & first, 1.0, 0.0),
                axis=1, keepdims=True,
            )
        slot_row.append(jnp.where(rank_row < CAP, e_row[k] * CAP + rank_row, -1.0))
        slot_col.append(jnp.where(rank_col < CAP, e_col[k] * CAP + rank_col, -1.0))

    lane_64 = lax.broadcasted_iota(jnp.int32, (128, 64), 1)
    row_128 = lax.broadcasted_iota(jnp.int32, (128, 64), 0)
    row_expert = lax.bitwise_xor(lax.div(row_128, 16), jnp.full_like(row_128, me))
    row_slot = (row_expert * CAP + lax.rem(row_128, 4)).astype(F32)
    same_part = lax.rem(lax.div(row_128, 4), 4) == lax.div(lane_64, ROWS)
    dispatch = jnp.where(
        same_part & ((slot_row[0] == row_slot) | (slot_row[1] == row_slot)), 1.0, 0.0
    ).astype(BF)
    row_64 = lax.broadcasted_iota(jnp.int32, (64, 64), 0)
    col_64 = lax.broadcasted_iota(jnp.int32, (64, 64), 1)
    swapped = lax.rem(lax.div(row_64, 4), 4) * 16 + lax.div(row_64, 16) * 4 + lax.rem(row_64, 4)
    swap = jnp.where(col_64 == swapped, 1.0, 0.0).astype(BF)

    def score(h, block):
        return lax.dot_general(
            q_ref[:, h * HD : (h + 1) * HD], block, (((1,), (1,)), ((), ())),
            preferred_element_type=F32,
        )

    for h in range(HEADS_HERE):
        own_scores[h] = score(h, k_ref[...])
    pl.semaphore_wait(barrier, len(greeted))

    kv_copies = []
    for which, ref in enumerate((k_ref, v_ref)):
        for back_steps in (1, 2):
            slot = which * 2 + back_steps - 1
            copy = remote(ref, kv.at[slot], kv_s.at[slot], kv_r.at[slot], after(back_steps))
            copy.start()
            kv_copies.append(copy)
    for copy in weight_copies:
        copy.start()

    head_copies = []
    for group in range(GROUPS):
        weights, denominators = [], []
        for h in range(group * GROUP_HEADS, (group + 1) * GROUP_HEADS):
            if h == 0:
                kv_copies[0].wait_recv()
                kv_copies[1].wait_recv()
            scores = jnp.concatenate(
                [score(h, kv[1]), score(h, kv[0]), own_scores[h]], axis=1
            ) * HD ** (-0.5)
            scores = jnp.where(visible, scores, MASKED)
            highest = jnp.max(scores, axis=1, keepdims=True)
            weight = jnp.where(visible, jnp.exp(scores - highest), 0.0)
            denominators.append(jnp.sum(weight, axis=1, keepdims=True))
            weights.append(weight.astype(BF))
        if group == 0:
            kv_copies[2].wait_recv()
            kv_copies[3].wait_recv()
        for n in range(GROUP_HEADS):
            total = dot(weights[n][:, :TOK], kv[3])
            total += dot(weights[n][:, TOK : 2 * TOK], kv[2])
            total += dot(weights[n][:, 2 * TOK :], v_ref[...])
            head = (total / denominators[n]).astype(BF)
            heads[group, :, :, n * HD : (n + 1) * HD] = head.reshape(EXP, ROWS, HD)
        for d in range(1, EXP):
            copy = remote(
                heads.at[group, partner(d)], held.at[group, me],
                hd_s.at[group, d], hd_r.at[group, d], ring(0, d),
            )
            copy.start()
            head_copies.append(copy)
        held[group, me] = heads[group, me]

    for copy in head_copies:
        copy.wait_recv()
    square = jnp.zeros((ROWS, 1), F32)
    for e in range(EXP):
        for group in range(GROUPS):
            block = held[group, e].astype(F32)
            square += jnp.sum(block * block, axis=1, keepdims=True)
    inverse = lax.rsqrt(square * (1.0 / D) + EPS)
    gain = gain_ref[...].astype(F32)
    for n in range(D // HD):
        e, h = n // HEADS_HERE, n % HEADS_HERE
        first_lane = h % GROUP_HEADS * HD
        block = held[h // GROUP_HEADS, e, :, first_lane : first_lane + HD].astype(F32)
        block = block * inverse * gain[n : n + 1, :]
        part, column = n // 12, n % 12 * HD
        normed[part * ROWS : (part + 1) * ROWS, column : column + HD] = block.astype(BF)

    sends[...] = dot(dispatch, normed[...]).astype(BF).reshape(EXP, 16, WIDE)
    slot_copies = {}

    def send_slots(far):
        for d in range(EXP):
            if not far and not d:
                continue
            n = far * EXP + d
            copy = remote(sends.at[d], arrived.at[n], ds_s.at[n], ds_r.at[n], ring(far, d))
            copy.start()
            slot_copies[n] = copy

    send_slots(0)
    arrived[0] = sends[0]

    def make_blend():
        logits = jnp.zeros((ROWS, EXP), F32)
        for part in range(PARTS):
            logits += lax.dot_general(
                normed[part * ROWS : (part + 1) * ROWS, :],
                router_ref[:, part * WIDE : (part + 1) * WIDE],
                (((1,), (1,)), ((), ())), preferred_element_type=F32,
            )
        lane_8 = lax.broadcasted_iota(jnp.int32, (ROWS, EXP), 1).astype(F32)
        picked = [
            jnp.sum(jnp.where(lane_8 == e, logits, 0.0), axis=1, keepdims=True) for e in e_col
        ]
        shares = [
            1.0 / (1.0 + jnp.exp(picked[1] - picked[0])),
            1.0 / (1.0 + jnp.exp(picked[0] - picked[1])),
        ]
        lane_256 = lax.broadcasted_iota(jnp.int32, (64, 256), 1)
        row_b = lax.broadcasted_iota(jnp.int32, (64, 256), 0)
        lane_expert = lax.bitwise_xor(
            lax.rem(lax.div(lane_256, 16), EXP), jnp.full_like(lane_256, me)
        )
        lane_slot = (lane_expert * CAP + lax.rem(lane_256, 4)).astype(F32)
        blend = jnp.zeros((64, 256), F32)
        for k in range(2):
            slot_tall = jnp.concatenate([slot_col[k]] * PARTS, axis=0)
            share_tall = jnp.concatenate([shares[k]] * PARTS, axis=0)
            blend += jnp.where(slot_tall == lane_slot, share_tall, 0.0)
        blend_ref[...] = jnp.where(
            lax.div(row_b, ROWS) == lax.rem(lax.div(lane_256, 4), 4), blend, 0.0
        )

    axes = [("x", "y"), ("y", "x"), ("x", "y"), ("y", "x")]
    first_sign = [1, -1, -1, 1]

    def second_sign(a):
        return 1 if a < 2 else -1

    def at(a, b):
        return a * 4 + b

    copies = {}

    def gather_copy(k, slot):
        a, b = divmod(slot, 4)
        if b:
            axis = axes[k][1]
            if b == 2:
                sign = second_sign(a)
                src = at(a, 3 if sign > 0 else 1)
            else:
                sign = 1 if b == 3 else -1
                src = at(a, 0)
        else:
            axis = axes[k][0]
            if a == 2:
                sign = first_sign[k]
                src = at(3 if sign > 0 else 1, 0)
            else:
                sign = 1 if a == 3 else -1
                src = 0
        if k >= 2 and b == 2 and a in CROSSING:
            src_ref, device = tokens.at[k - 2, slot], (other_ctx, me)
        else:
            src_ref, device = tokens.at[k, src], near(axis, sign)
        return remote(src_ref, tokens.at[k, slot], ag_s.at[k, slot], ag_r.at[k, slot], device)

    def sum_copy(k, c, n):
        if n < 12:
            a, kind = divmod(n, 3)
            axis, sign = axes[k][1], second_sign(a)
            ahead, behind = (1, 3) if sign > 0 else (3, 1)
            src = at(a, (2, ahead, behind)[kind])
        else:
            kind, axis, sign = n - 12, axes[k][0], first_sign[k]
            ahead, behind = (1, 3) if sign > 0 else (3, 1)
            src = at((2, ahead, behind)[kind], 0)
        return remote(
            parts.at[k, c, src], landed.at[k, c, n], rs_s.at[k, c, n], rs_r.at[k, c, n],
            near(axis, -sign if kind == 2 else sign),
        )

    def over_copy(k, c, a):
        n = OVER.index(a)
        return remote(
            parts.at[k, c, at(a, 2)], crossed.at[k, c, n], ov_s.at[k, c, n], ov_r.at[k, c, n],
            (other_ctx, me),
        )

    makers = {"gather": gather_copy, "sum": sum_copy, "over": over_copy}
    waited = set()

    def copy_of(*key):
        if key not in copies:
            copies[key] = makers[key[0]](*key[1:])
        return copies[key]

    def arrival(*key):
        if key not in waited:
            waited.add(key)
            copy_of(*key).wait_recv()

    def take_slots(k):
        first_n = (k // 2) * EXP + (k % 2) * 4
        for n in range(first_n, first_n + 4):
            if n:
                slot_copies[n].wait_recv()
        rows = arrived[first_n : first_n + 4].reshape(64, WIDE)
        moved = dot(swap, rows).astype(BF)
        for part in range(PARTS):
            tokens[k, 0, :, part * WIDE : (part + 1) * WIDE] = moved[part * 16 : (part + 1) * 16]

    def own(k):
        take_slots(k)
        copy_of("gather", k, at(3, 0)).start()
        copy_of("gather", k, at(1, 0)).start()
        if k == 1:
            send_slots(1)
            make_blend()

    def spread(k, a):
        if a:
            arrival("gather", k, at(a, 0))
        copy_of("gather", k, at(a, 3)).start()
        copy_of("gather", k, at(a, 1)).start()

    def forward(k):
        arrival("gather", k, at(3 if first_sign[k] > 0 else 1, 0))
        copy_of("gather", k, at(2, 0)).start()

    def onward(k, a):
        arrival("gather", k, at(a, 3 if second_sign(a) > 0 else 1))
        copy_of("gather", k, at(a, 2)).start()

    def cross(k, a):
        arrival("gather", k - 2, at(a, 2))
        copy_of("gather", k, at(a, 2)).start()

    def ffn(k, n):
        if n == 0:
            for slot in range(1, 16):
                arrival("gather", k, slot)
            if k == 0:
                for copy in weight_copies:
                    copy.wait()
        if n < PARTS:
            columns = slice(n * WIDE, (n + 1) * WIDE)
            rows = tokens[k, :, :, columns].reshape(256, WIDE)
            gate = dot(rows, gate_w[columns, :])
            up = dot(rows, up_w[columns, :])
            if n:
                gate = gate_acc[...] + gate
                up = up_acc[...] + up
            if n == PARTS - 1:
                hidden[...] = (gate / (1.0 + jnp.exp(-gate)) * up).astype(BF)
            else:
                gate_acc[...] = gate
                up_acc[...] = up
        else:
            column = (n - PARTS) * WIDE
            first_column = column % HALF
            parts[k, column // HALF, :, :, first_column : first_column + WIDE] = (
                dot(hidden[...], down_w[:, column : column + WIDE])
                .astype(BF).reshape(16, 16, WIDE)
            )

    def add(k, c, slot, *ns):
        total = parts[k, c, slot].astype(F32)
        for n in ns:
            arrival("sum", k, c, n)
            total += landed[k, c, n].astype(F32)
        parts[k, c, slot] = total.astype(BF)

    def over(k, c, a):
        copy_of("over", k, c, a).start()

    def far(k, c, a):
        if k >= 2 and a in OVER:
            arrival("over", k - 2, c, a)
            total = parts[k, c, at(a, 2)].astype(F32)
            total += crossed[k - 2, c, OVER.index(a)].astype(F32)
            parts[k, c, at(a, 2)] = total.astype(BF)
        copy_of("sum", k, c, a * 3).start()

    def side(k, c, a):
        copy_of("sum", k, c, a * 3 + 2).start()

    def middle(k, c, a):
        if k >= 2 or a not in OVER:
            add(k, c, at(a, 1 if second_sign(a) > 0 else 3), a * 3)
        copy_of("sum", k, c, a * 3 + 1).start()

    def close(k, c, a):
        ahead = 1 if first_sign[k] > 0 else 3
        more = {2: (), ahead: (12,), 4 - ahead: (), 0: (13, 14)}[a]
        add(k, c, at(a, 0), a * 3 + 1, a * 3 + 2, *more)
        if a:
            copy_of("sum", k, c, {2: 12, ahead: 13, 4 - ahead: 14}[a]).start()

    rt = {}

    def give(k, c):
        rows = jnp.concatenate(
            [parts[k, c, 0, :, n * NARROW : (n + 1) * NARROW] for n in range(PARTS)], axis=0
        )
        back[k, c] = dot(swap, rows).astype(BF).reshape(4, 16, NARROW)
        for m in range(4):
            d = (k % 2) * 4 + m
            n = (k // 2) * EXP + d
            if n:
                copy = remote(
                    back.at[k, c, m], returned.at[c, n], rt_s.at[c, n], rt_r.at[c, n],
                    ring(k // 2, d),
                )
                copy.start()
                rt[c, n] = copy
            else:
                returned[c, 0] = back[k, c, m]

    steps = [own, spread, forward, onward, cross, ffn, over, far, side, middle, close, give]
    for which, *where in ORDER:
        steps[which](*where)

    high = blend_ref[...].astype(BF)
    low = (blend_ref[...] - high.astype(F32)).astype(BF)
    for c in range(HALVES):
        for n in range(1, 2 * EXP):
            rt[c, n].wait_recv()
        came = returned[c].reshape(256, NARROW)
        mixed = dot(high, came) + dot(low, came)
        for part in range(PARTS):
            e = c * PARTS + part
            for group in range(GROUPS):
                columns = slice(group * GROUP_COLS, (group + 1) * GROUP_COLS)
                block = mixed[part * ROWS : (part + 1) * ROWS, columns]
                first_column = e * COLS + group * GROUP_COLS
                out_ref[:, first_column : first_column + GROUP_COLS] = (
                    held[group, e].astype(F32) + block
                ).astype(BF)

    for copy in kv_copies + head_copies + list(slot_copies.values()) + list(rt.values()):
        copy.wait_send()
    for copy in copies.values():
        copy.wait_send()


def body(
    queries, keys, values, span_order, norm_gain, router_weight, routes, priority,
    w_gate, w_up, w_down,
):
    vmem = pl.BlockSpec(memory_space=pltpu.VMEM)
    smem = pl.BlockSpec(memory_space=pltpu.SMEM)
    hbm = pl.BlockSpec(memory_space=pl.ANY)
    dma = pltpu.SemaphoreType.DMA
    return pl.pallas_call(
        kernel,
        out_shape=jax.ShapeDtypeStruct((ROWS, D), BF),
        in_specs=[vmem, vmem, vmem, smem, vmem, vmem, vmem, vmem, hbm, hbm, hbm],
        out_specs=vmem,
        scratch_shapes=[
            pltpu.VMEM((4, TOK, HD), BF),
            pltpu.VMEM((HEADS_HERE, TOK, TOK), F32),
            pltpu.VMEM((GROUPS, EXP, ROWS, GROUP_COLS), BF),
            pltpu.VMEM((GROUPS, EXP, ROWS, GROUP_COLS), BF),
            pltpu.VMEM((64, WIDE), BF),
            pltpu.VMEM((EXP, 16, WIDE), BF),
            pltpu.VMEM((2 * EXP, 16, WIDE), BF),
            pltpu.VMEM((4, 16, 16, D), BF),
            pltpu.VMEM((D, HID), BF),
            pltpu.VMEM((D, HID), BF),
            pltpu.VMEM((HID, D), BF),
            pltpu.VMEM((256, HID), F32),
            pltpu.VMEM((256, HID), F32),
            pltpu.VMEM((256, HID), BF),
            pltpu.VMEM((4, HALVES, 16, 16, HALF), BF),
            pltpu.VMEM((4, HALVES, 15, 16, HALF), BF),
            pltpu.VMEM((2, HALVES, len(OVER), 16, HALF), BF),
            pltpu.VMEM((4, HALVES, 4, 16, NARROW), BF),
            pltpu.VMEM((HALVES, 2 * EXP, 16, NARROW), BF),
            pltpu.VMEM((64, 256), F32),
            dma((4,)), dma((4,)),
            dma((GROUPS, EXP)), dma((GROUPS, EXP)),
            dma((2 * EXP,)), dma((2 * EXP,)),
            dma((4, 16)), dma((4, 16)),
            dma((4, HALVES, 15)), dma((4, HALVES, 15)),
            dma((2, HALVES, len(OVER))), dma((2, HALVES, len(OVER))),
            dma((HALVES, 2 * EXP)), dma((HALVES, 2 * EXP)),
            dma((3,)),
        ],
        compiler_params=pltpu.CompilerParams(
            collective_id=0, has_side_effects=True, vmem_limit_bytes=60 * 1024 * 1024
        ),
    )(
        queries, keys, values, span_order, norm_gain.reshape(D // HD, HD),
        router_weight.T, routes.T, priority, w_gate, w_up, w_down,
    )


def solution(mesh):
    placed = (
        P("ctx", "exp"),
        P("ctx", "exp"),
        P("ctx", "exp"),
        P(),
        P(),
        P(),
        P(("ctx", "exp"), None),
        P(("ctx", "exp"), None),
        P("exp", None, "ctx"),
        P("exp", None, "ctx"),
        P("exp", "ctx", None),
    )
    return jax.shard_map(
        body, mesh=mesh, in_specs=placed, out_specs=P(("ctx", "exp"), None), check_vma=False
    )
```

time: 211 us -> 183 us (0.87)
  Pallas kernels: 204 us -> 182 us
  local copies, waits for them, and re-layouts: 5.23 us -> 1.62 us
    pallas_call x1, Pallas kernels: 204 us -> 182 us  [body(): pl.pallas_call(kernel, out_shape=jax.ShapeDtypeStruct((ROWS, D), BF), in_...]
    unnamed x3 -> x1, local copies, waits for them, and re-layouts: 5.23 us -> 1.62 us
where the time goes in v2:
time: 183 us
  Pallas kernels  182 us (99%)
    pallas_call x1, Pallas kernels, body(): pl.pallas_call(kernel, out_shape=jax.ShapeDtypeStruct((ROWS, D), BF), in_...  182 us

profile of v2, /device:TPU:1, one launch (start us, length us, event | category | flops | bytes accessed | tf_op | source)
XLA Modules:
  0.0 183.3 jit_solution(16112543380120749964)
XLA Ops:
  0.0 181.7 %shard_map.109 = bf16[16,6144]{1,0:T(8,128)(2,1)} custom-call(bf16[128,768]{1,0:T(8,128)(2,1)} %q_ref.1, bf16[128,128]{1,0:T(8,128)(2,1)} %k_ref.1, bf16[128,128]{1,0:T(8,128)(2,1)} %v_ref.1, s32[64]{0:T(128)} %span_ref.1, bf16[48,128]{1,0:T(8,128)(2,1)} %bitcast.4, bf16[8,6144]{1,0:T(8,128)(2,1)} %bitcast.3, s32[2,16]{1,0:T(2,128)} %bitcast.5, ...), custom_call_target="tpu_custom_call" | custom-call | tf_op jit(solution)/shard_map/pallas_call | solution.py:532
  181.7 1.6 copy.13

commit v3 on v2

--- a/solution.py
+++ b/solution.py
@@ -31,37 +31,37 @@
 CROSSING = (0, 3)
 OVER = (2, 1)
 ORDER = (
-    (0, 0), (1, 0, 0), (2, 0), (1, 0, 3), (0, 1), (1, 1, 0), (1, 0, 1), (1, 0, 2), (3, 1, 0),
-    (2, 1), (1, 1, 3), (1, 1, 1), (3, 0, 0), (0, 2), (0, 3), (1, 2, 0), (1, 3, 0), (4, 3, 0),
-    (3, 1, 3), (4, 2, 0), (1, 1, 2), (3, 0, 3), (3, 0, 1), (2, 2), (1, 2, 1), (2, 3), (1, 3, 1),
-    (1, 3, 3), (1, 2, 3), (4, 3, 3), (4, 2, 3), (3, 0, 2), (3, 1, 1), (3, 2, 1), (1, 2, 2),
-    (3, 3, 1), (3, 1, 2), (1, 3, 2), (5, 0, 0), (5, 0, 1), (5, 0, 2), (5, 0, 3), (5, 0, 4),
-    (5, 0, 5), (5, 0, 6), (5, 0, 7), (9, 0, 1, 2), (9, 0, 0, 2), (9, 0, 1, 1), (9, 0, 0, 1),
-    (7, 0, 1, 3), (7, 0, 0, 3), (7, 0, 1, 0), (7, 0, 0, 0), (6, 0, 1, 2), (6, 0, 0, 2),
-    (6, 0, 1, 1), (6, 0, 0, 1), (3, 2, 2), (5, 1, 0), (5, 1, 1), (5, 1, 2), (5, 1, 3), (5, 1, 4),
-    (5, 1, 5), (9, 1, 0, 2), (5, 1, 6), (5, 1, 7), (9, 1, 1, 2), (9, 1, 1, 1), (9, 1, 0, 1),
-    (7, 1, 1, 3), (7, 1, 0, 3), (8, 0, 1, 2), (8, 1, 1, 2), (8, 1, 0, 2), (7, 1, 1, 0),
-    (7, 1, 0, 0), (8, 0, 1, 1), (6, 1, 1, 2), (6, 1, 0, 2), (6, 1, 1, 1), (6, 1, 0, 1), (3, 3, 2),
-    (8, 0, 0, 2), (9, 0, 1, 3), (8, 0, 1, 3), (9, 0, 0, 3), (9, 0, 1, 0), (8, 1, 1, 1),
-    (8, 1, 1, 3), (8, 0, 0, 1), (9, 1, 1, 3), (9, 0, 0, 0), (10, 1, 1, 2), (5, 2, 0), (5, 2, 1),
-    (9, 1, 0, 3), (5, 2, 2), (5, 2, 3), (5, 2, 4), (5, 2, 5), (5, 2, 6), (5, 2, 7), (7, 2, 1, 2),
-    (9, 1, 1, 0), (7, 2, 0, 2), (7, 2, 1, 3), (8, 1, 0, 3), (8, 0, 0, 3), (8, 1, 0, 1),
-    (7, 2, 0, 3), (8, 2, 1, 2), (10, 0, 1, 2), (10, 0, 0, 2), (5, 3, 0), (5, 3, 1), (9, 1, 0, 0),
-    (5, 3, 2), (5, 3, 3), (5, 3, 4), (5, 3, 5), (5, 3, 6), (5, 3, 7), (7, 2, 1, 1), (7, 3, 1, 3),
-    (7, 3, 0, 3), (8, 2, 0, 2), (10, 1, 0, 2), (7, 2, 1, 0), (7, 3, 1, 0), (7, 2, 0, 0),
-    (7, 3, 0, 0), (8, 1, 1, 0), (10, 0, 1, 3), (10, 1, 1, 1), (10, 1, 1, 3), (10, 0, 0, 3),
-    (9, 2, 1, 2), (10, 1, 0, 1), (7, 2, 0, 1), (10, 0, 1, 1), (9, 2, 0, 2), (9, 3, 1, 3),
-    (9, 2, 1, 1), (10, 0, 0, 1), (9, 2, 1, 3), (9, 3, 0, 3), (7, 3, 1, 2), (9, 2, 0, 3),
-    (8, 3, 1, 2), (9, 2, 1, 0), (9, 3, 1, 0), (10, 1, 0, 3), (9, 2, 0, 0), (8, 1, 0, 0),
-    (9, 3, 0, 0), (7, 3, 0, 2), (10, 1, 1, 0), (11, 1, 1), (10, 2, 1, 2), (8, 3, 0, 2),
-    (8, 0, 1, 0), (8, 2, 1, 3), (10, 2, 0, 2), (8, 3, 1, 3), (8, 0, 0, 0), (9, 2, 0, 1),
-    (7, 3, 1, 1), (8, 2, 1, 1), (9, 3, 1, 2), (8, 2, 0, 3), (8, 3, 0, 3), (8, 2, 0, 1),
-    (8, 3, 1, 1), (10, 1, 0, 0), (11, 1, 0), (9, 3, 0, 2), (7, 3, 0, 1), (8, 2, 1, 0),
-    (10, 0, 1, 0), (11, 0, 1), (8, 2, 0, 0), (10, 2, 1, 3), (10, 3, 1, 3), (10, 0, 0, 0),
-    (11, 0, 0), (8, 3, 0, 1), (9, 3, 1, 1), (10, 2, 1, 1), (10, 3, 1, 2), (10, 2, 0, 3),
-    (10, 3, 0, 3), (10, 2, 0, 1), (8, 3, 1, 0), (9, 3, 0, 1), (10, 3, 0, 2), (8, 3, 0, 0),
-    (10, 3, 1, 1), (10, 2, 1, 0), (11, 2, 1), (10, 2, 0, 0), (11, 2, 0), (10, 3, 0, 1),
-    (10, 3, 1, 0), (11, 3, 1), (10, 3, 0, 0), (11, 3, 0),
+    (0, 0), (1, 0, 0), (0, 1), (3, 0, 0), (1, 1, 0), (2, 0), (1, 0, 1), (1, 1, 1), (2, 1),
+    (3, 1, 0), (1, 1, 3), (0, 2), (1, 0, 3), (0, 3), (4, 2, 0), (3, 0, 1), (1, 0, 2), (1, 1, 2),
+    (3, 0, 3), (4, 3, 0), (2, 2), (3, 1, 1), (3, 0, 2), (3, 1, 3), (1, 3, 3), (2, 3), (1, 2, 2),
+    (3, 1, 2), (1, 2, 1), (1, 3, 1), (4, 2, 3), (5, 0, 0), (5, 0, 1), (4, 3, 3), (1, 3, 2),
+    (5, 0, 2), (5, 0, 3), (5, 0, 4), (1, 2, 3), (5, 0, 5), (5, 0, 6), (9, 0, 0, 2), (3, 2, 1),
+    (1, 2, 0), (5, 0, 7), (5, 1, 0), (6, 0, 0, 1), (5, 1, 1), (3, 3, 1), (5, 1, 2), (5, 1, 3),
+    (5, 1, 4), (5, 1, 5), (1, 3, 0), (8, 0, 1, 3), (7, 1, 0, 3), (8, 1, 0, 0), (8, 0, 0, 2),
+    (3, 2, 2), (5, 1, 6), (7, 0, 1, 3), (5, 1, 7), (7, 1, 0, 0), (3, 3, 2), (7, 0, 0, 0),
+    (9, 1, 0, 2), (8, 1, 1, 2), (7, 0, 0, 3), (8, 0, 0, 1), (8, 0, 1, 0), (8, 1, 0, 1),
+    (6, 1, 0, 2), (9, 1, 0, 1), (8, 1, 0, 2), (8, 0, 1, 1), (9, 1, 0, 0), (7, 1, 1, 0), (5, 2, 0),
+    (5, 2, 1), (9, 1, 0, 3), (9, 0, 0, 1), (8, 1, 0, 3), (8, 0, 1, 2), (5, 2, 2), (8, 0, 0, 3),
+    (5, 2, 3), (6, 1, 0, 1), (5, 2, 4), (9, 0, 0, 0), (7, 0, 1, 0), (5, 2, 5), (9, 0, 1, 1),
+    (7, 1, 1, 3), (5, 2, 6), (5, 2, 7), (5, 3, 0), (6, 1, 1, 2), (8, 2, 1, 2), (5, 3, 1),
+    (9, 0, 1, 3), (10, 0, 0, 2), (5, 3, 2), (5, 3, 3), (5, 3, 4), (5, 3, 5), (6, 0, 0, 2),
+    (8, 2, 0, 1), (6, 0, 1, 2), (7, 3, 0, 3), (8, 3, 0, 2), (8, 3, 0, 0), (10, 1, 0, 1),
+    (7, 3, 0, 2), (7, 2, 1, 0), (5, 3, 6), (7, 2, 0, 3), (10, 1, 0, 2), (8, 3, 0, 3), (5, 3, 7),
+    (8, 3, 1, 2), (8, 2, 1, 3), (9, 0, 0, 3), (6, 1, 1, 1), (6, 0, 1, 1), (9, 3, 0, 3),
+    (8, 3, 0, 1), (8, 2, 0, 2), (9, 0, 1, 2), (9, 3, 0, 2), (7, 3, 1, 2), (8, 3, 1, 3),
+    (8, 3, 1, 0), (10, 0, 0, 3), (7, 3, 0, 1), (8, 2, 0, 3), (10, 1, 0, 3), (7, 3, 0, 0),
+    (10, 0, 1, 2), (10, 3, 0, 3), (7, 2, 0, 1), (7, 2, 0, 2), (7, 3, 1, 0), (9, 0, 1, 0),
+    (8, 2, 0, 0), (9, 3, 1, 2), (7, 3, 1, 3), (10, 3, 0, 2), (7, 2, 1, 2), (9, 3, 0, 1),
+    (7, 2, 1, 3), (9, 3, 0, 0), (9, 1, 1, 2), (10, 0, 1, 3), (9, 2, 0, 1), (9, 2, 0, 2),
+    (10, 3, 1, 2), (8, 0, 0, 0), (8, 3, 1, 1), (7, 3, 1, 1), (10, 0, 1, 1), (10, 1, 0, 0),
+    (9, 3, 1, 3), (10, 3, 0, 1), (8, 2, 1, 1), (11, 1, 0), (10, 0, 0, 1), (7, 2, 1, 1),
+    (9, 2, 1, 2), (10, 2, 0, 2), (9, 3, 1, 1), (9, 2, 0, 3), (10, 3, 0, 0), (7, 2, 0, 0),
+    (9, 2, 1, 3), (9, 1, 1, 1), (8, 1, 1, 1), (10, 0, 0, 0), (10, 0, 1, 0), (11, 3, 0),
+    (10, 3, 1, 3), (10, 2, 1, 2), (9, 2, 1, 1), (9, 3, 1, 0), (10, 1, 1, 2), (11, 0, 1),
+    (10, 2, 0, 3), (10, 3, 1, 1), (11, 0, 0), (8, 2, 1, 0), (8, 1, 1, 3), (9, 2, 0, 0),
+    (9, 1, 1, 3), (9, 2, 1, 0), (10, 2, 0, 1), (10, 2, 1, 3), (10, 2, 1, 1), (9, 1, 1, 0),
+    (10, 3, 1, 0), (10, 1, 1, 1), (8, 1, 1, 0), (11, 3, 1), (10, 2, 0, 0), (11, 2, 0),
+    (10, 1, 1, 3), (10, 2, 1, 0), (11, 2, 1), (10, 1, 1, 0), (11, 1, 1),
 )
 EPS = 1e-05
 MASKED = -1e30

time: 183 us -> 176 us (0.962)
  Pallas kernels: 182 us -> 175 us
    pallas_call x1, Pallas kernels: 182 us -> 175 us  [body(): pl.pallas_call(kernel, out_shape=jax.ShapeDtypeStruct((ROWS, D), BF), in_...]
where the time goes in v3:
time: 176 us
  Pallas kernels  175 us (99%)
    pallas_call x1, Pallas kernels, body(): pl.pallas_call(kernel, out_shape=jax.ShapeDtypeStruct((ROWS, D), BF), in_...  175 us

profile of v3, /device:TPU:1, one launch (start us, length us, event | category | flops | bytes accessed | tf_op | source)
XLA Modules:
  0.0 176.2 jit_solution(9825739125816932627)
XLA Ops:
  0.0 174.6 %shard_map.109 = bf16[16,6144]{1,0:T(8,128)(2,1)} custom-call(bf16[128,768]{1,0:T(8,128)(2,1)} %q_ref.1, bf16[128,128]{1,0:T(8,128)(2,1)} %k_ref.1, bf16[128,128]{1,0:T(8,128)(2,1)} %v_ref.1, s32[64]{0:T(128)} %span_ref.1, bf16[48,128]{1,0:T(8,128)(2,1)} %bitcast.4, bf16[8,6144]{1,0:T(8,128)(2,1)} %bitcast.3, s32[2,16]{1,0:T(2,128)} %bitcast.5, ...), custom_call_target="tpu_custom_call" | custom-call | tf_op jit(solution)/shard_map/pallas_call | solution.py:532
  174.6 1.6 copy.13

commit v4 on v3

--- a/solution.py
+++ b/solution.py
@@ -391,8 +391,9 @@
         take_slots(k)
         copy_of("gather", k, at(3, 0)).start()
         copy_of("gather", k, at(1, 0)).start()
+        if k == 0:
+            send_slots(1)
         if k == 1:
-            send_slots(1)
             make_blend()
 
     def spread(k, a):

time: 176 us -> 177 us (level)
  no operation moved by 1% of the time
where the time goes in v4:
time: 177 us
  Pallas kernels  176 us (99%)
    pallas_call x1, Pallas kernels, body(): pl.pallas_call(kernel, out_shape=jax.ShapeDtypeStruct((ROWS, D), BF), in_...  176 us

profile of v4, /device:TPU:1, one launch (start us, length us, event | category | flops | bytes accessed | tf_op | source)
XLA Modules:
  0.0 177.3 jit_solution(12368992615062651907)
XLA Ops:
  0.0 175.7 %shard_map.109 = bf16[16,6144]{1,0:T(8,128)(2,1)} custom-call(bf16[128,768]{1,0:T(8,128)(2,1)} %q_ref.1, bf16[128,128]{1,0:T(8,128)(2,1)} %k_ref.1, bf16[128,128]{1,0:T(8,128)(2,1)} %v_ref.1, s32[64]{0:T(128)} %span_ref.1, bf16[48,128]{1,0:T(8,128)(2,1)} %bitcast.4, bf16[8,6144]{1,0:T(8,128)(2,1)} %bitcast.3, s32[2,16]{1,0:T(2,128)} %bitcast.5, ...), custom_call_target="tpu_custom_call" | custom-call | tf_op jit(solution)/shard_map/pallas_call | solution.py:533
  175.7 1.6 copy.13
